TPU v7x, 512 devices: a whole 4x4x16 slice. The times are simulated.
512 devices in a mesh: row: 32 (over z_lo, y, core), col: 16 (over z_hi, x).
Axes of the slice: x: 4, y: 4, z: 16 (z_hi: 4, z_lo: 4; z = z_hi * 4 + z_lo), core: 2. Of those that a mesh axis runs over, the one named last changes fastest.
Arguments:
- iterate: float32 [3584, 14336], P('row', 'col'), may hold values from -0.040089186 to 0.040089186
Outputs:
- update: bfloat16 [3584, 14336], P('row', 'col')
All inputs are finite; a program needn't handle non-finite values.
Results may differ from a plain program's by a relative error of at most 0.04.
Values may be sent and summed in bfloat16 or wider, within the bound.
A program may use at most 64 MiB of HBM per device.

v0:
```python
import math

import jax
import jax.numpy as jnp
from jax import lax
from jax.sharding import PartitionSpec as P

N = 14336


def body(iterate):
    iterate_b = iterate.astype(jnp.bfloat16)
    partial_gram = lax.dot_general(
        lax.all_gather(iterate_b, "row", axis=0, tiled=True),
        iterate_b,
        (((1,), (1,)), ((), ())),
        preferred_element_type=jnp.float32,
    )
    gram_share = lax.psum_scatter(
        partial_gram.astype(jnp.bfloat16), "col", scatter_dimension=0, tiled=True
    ).astype(jnp.float32)
    gram_column = lax.all_gather(gram_share.astype(jnp.bfloat16), "col", axis=0, tiled=True)
    share_b = gram_share.astype(jnp.bfloat16)
    square = jnp.dot(
        lax.all_gather(share_b, "row", axis=1, tiled=True),
        gram_column,
        preferred_element_type=jnp.float32,
    )
    poly = (-4.775 * gram_share + 2.0315 * square).astype(jnp.bfloat16)
    poly_column = lax.all_gather(poly, "col", axis=0, tiled=True)
    product = lax.dot_general(
        poly_column,
        lax.all_gather(iterate_b, "row", axis=0, tiled=True),
        (((0,), (0,)), ((), ())),
        preferred_element_type=jnp.float32,
    )
    scale = 0.2 * math.sqrt(N)
    return (scale * (3.4445 * iterate + product)).astype(jnp.bfloat16)


def solution(mesh):
    placed = (P("row", "col"),)
    return jax.shard_map(
        body, mesh=mesh, in_specs=placed, out_specs=P("row", "col"), check_vma=False
    )
```

profile of v0, /device:TPU:1, one launch (start us, length us, event | category | flops | bytes accessed | tf_op | source)
XLA Modules:
  0.0 349.2 jit_solution(3531867230818866686)
XLA Ops:
  6.5 0.0 all-gather.3.cloned.1.call-start
  6.5 1.7 convert_element_type.17
  8.2 0.0 all-gather.3.cloned.1.call-update
  8.3 0.0 copy-start
  8.3 0.0 reduce-scatter.2.cloned.1.call-start
  8.3 78.5 %all-gather.3.cloned.1.call-done = bf16[3584,896]{1,0:T(8,128)(2,1)} async-done(((bf16[112,896]{1,0:T(8,128)(2,1)}), bf16[3584,896]{1,0:T(8,128)(2,1)}) %all-gather.3.cloned.1.call-update) | async-done | bytes 6422544 | tf_op jit(solution)/shard_map/all_gather | solution.py:14
  86.8 5.6 %convolution_convert_fusion = bf16[3584,112]{1,0:T(8,128)(2,1)} fusion(bf16[3584,896]{1,0:T(8,128)(2,1)} %all-gather.3.cloned.1.call-done, bf16[112,896]{1,0:T(8,128)(2,1)} %convert_element_type.17), kind=kOutput, calls=%fused_computation | convolution fusion | flops 719724544 | bytes 7426048 | tf_op jit(solution)/shard_map/dot_general | solution.py:13
  92.4 0.0 reduce-scatter.2.cloned.1.call-update
  92.5 0.0 all-gather.5.cloned.1.call-start
  92.5 111.1 %reduce-scatter.2.cloned.1.call-done = bf16[224,112]{1,0:T(8,128)(2,1)} async-done(((bf16[3584,112]{1,0:T(8,128)(2,1)}), bf16[224,112]{1,0:T(8,128)(2,1)}) %reduce-scatter.2.cloned.1.call-update) | async-done | bytes 50192 | tf_op jit(solution)/shard_map/reduce_scatter | solution.py:19
  203.6 1.5 copy.2
  205.1 0.0 all-gather.5.cloned.1.call-update
  205.2 60.2 %all_gather.15 = bf16[3584,112]{1,0:T(8,128)(2,1)S(1)} all-gather(bf16[224,112]{1,0:T(8,128)(2,1)} %reduce-scatter.2.cloned.1.call-done), channel_id=1, replica_groups=mesh['row'=32,'col'=16] {'col'}, dimensions={0}, use_global_device_ids=true | all-gather | bytes 852992 | tf_op jit(solution)/shard_map/all_gather | solution.py:22
  265.3 8.3 %all-gather.5.cloned.1.call-done = bf16[224,3584]{0,1:T(8,128)(2,1)} async-done(((bf16[224,112]{0,1:T(8,128)(2,1)}), bf16[224,3584]{0,1:T(8,128)(2,1)}) %all-gather.5.cloned.1.call-update) | async-done | bytes 1605648 | tf_op jit(solution)/shard_map/all_gather | solution.py:25
  273.6 2.2 fusion.3
  275.8 62.3 %all_gather.16 = bf16[3584,112]{1,0:T(8,128)(2,1)S(1)} all-gather(bf16[224,112]{1,0:T(8,128)(2,1)S(1)} %fusion.3), channel_id=1, replica_groups=mesh['row'=32,'col'=16] {'col'}, dimensions={0}, use_global_device_ids=true | all-gather | bytes 852992 | tf_op jit(solution)/shard_map/all_gather | solution.py:30
  338.1 0.0 copy-done
  338.1 4.6 %fusion.1 = bf16[112,896]{1,0:T(8,128)(2,1)} fusion(bf16[3584,112]{1,0:T(8,128)(2,1)S(1)} %all_gather.16, bf16[3584,896]{1,0:T(8,128)(2,1)} %all-gather.3.cloned.1.call-done, f32[112,896]{1,0:T(8,128)S(1)} %copy-done), kind=kOutput, calls=%fused_computation.3 | convolution fusion | flops 719724544 | bytes 7827456 | tf_op jit(solution)/shard_map/dot_general | solution.py:31
Async XLA Ops:
  6.5 80.3 %all-gather.3.cloned.1.call-start = ((), (), s32[]{:S(2)}) async-start(), calls=%async_computation.1 | async-start | bytes 6623232 | tf_op jit(solution)/shard_map/all_gather | solution.py:14
  8.3 329.8 %copy-start = (f32[112,896]{1,0:T(8,128)S(1)}, f32[112,896]{1,0:T(8,128)}, u32[]{:S(2)}) copy-start(f32[112,896]{1,0:T(8,128)} %param.1) | copy-start | bytes 1204228
  8.3 195.3 %reduce-scatter.2.cloned.1.call-start = ((), (), s32[]{:S(2)}) async-start(), calls=%async_computation.2 | async-start | bytes 974848 | tf_op jit(solution)/shard_map/reduce_scatter | solution.py:19
  92.5 181.1 %all-gather.5.cloned.1.call-start = ((), (), s32[]{:S(2)}) async-start(), calls=%async_computation.3 | async-start | bytes 1892352 | tf_op jit(solution)/shard_map/all_gather | solution.py:25
Sparse Core Ops, SparseCore 0:
  9.5 77.2 all-gather.2
  92.6 110.9 reduce-scatter.1
  206.0 67.5 all-gather.4
where the time goes:
time: 354 us; the launch traced here: 349 us
  waiting for transfers between devices  198 us (56%)
  blocking collectives  122 us (34%)
  between operations  13.1 us (4%)
  matrix products  12.4 us (4%)
    reduce_scatter x1, waiting for transfers between devices, body(): lax.psum_scatter(partial_gram.astype(jnp.bfloat16), 'col', scatter_dimens...  111 us
    all_gather x1, waiting for transfers between devices, body(): lax.all_gather(iterate_b, 'row', axis=0, tiled=True)  78.5 us
    all_gather x1, blocking collectives, body(): poly_column = lax.all_gather(poly, 'col', axis=0, tiled=True)  62.3 us
    all_gather x1, blocking collectives, body(): lax.all_gather(gram_share.astype(jnp.bfloat16), 'col', axis=0, tiled=True)  60.2 us
    all_gather x1, waiting for transfers between devices, body(): lax.all_gather(share_b, 'row', axis=1, tiled=True)  8.27 us
  transfers between devices with their start and end apart: 3, of which 3 were waited for; matrix products, arithmetic and copies ran while one was open for 0% of the time, Pallas kernels for 0%

commit v1 on v0

v1 whole, which is shorter than its diff:
```python
import math

import jax
import jax.numpy as jnp
from jax import lax
from jax.experimental import pallas as pl
from jax.experimental.pallas import tpu as pltpu
from jax.sharding import PartitionSpec as P

N = 14336
R = 112
C = 896
W = 256
BF = jnp.bfloat16
F32 = jnp.float32


def dot(a, b):
    return jnp.dot(a, b, preferred_element_type=F32)


def dot_t(a, b):
    return lax.dot_general(a, b, (((1,), (1,)), ((), ())), preferred_element_type=F32)


def rows_of(k):
    return pl.ds(pl.multiple_of(k * R, 16), R)


def cols_of(h):
    return pl.ds(pl.multiple_of(h * W, W), W)


def kernel(
    x_ref, o_ref,
    a_buf, b_buf, gp, rx, zs, rz, gs, gr, gc, pr, ps, osend, ro,
    s_a, r_a, s_b, r_b, s_c, r_c, s_x, r_x, s_z, r_z, s_h, r_h, s_y, r_y,
    s_l, r_l, s_q, r_q, s_k, r_k, s_p, r_p, s_u, r_u, s_o, r_o,
):
    row = lax.axis_index("row")
    col = lax.axis_index("col")
    zl, y, k = row // 8, (row // 2) % 4, row % 2
    zh, x = col // 4, col % 4

    def at(zl=zl, y=y, k=k, zh=zh, x=x):
        return ((zl * 4 + y) * 2 + k, zh * 4 + x)

    def send(src, dst, s, r, device):
        copy = pltpu.make_async_remote_copy(
            src_ref=src, dst_ref=dst, send_sem=s, recv_sem=r,
            device_id=device, device_id_type=pl.DeviceIdType.MESH,
        )
        copy.start()
        sent.append(copy)

    def arrived(ref, s, r):
        pltpu.make_async_remote_copy(
            src_ref=ref, dst_ref=ref, send_sem=s, recv_sem=r,
            device_id=at(k=1 - k), device_id_type=pl.DeviceIdType.MESH,
        ).wait_recv()

    sent = []
    x_b = x_ref[...].astype(BF)
    a_buf[rows_of(y)] = x_b
    b_buf[zl, rows_of(k)] = x_b
    b_buf[:, 2 * R :] = jnp.zeros((4, W - 2 * R, C), BF)
    gc[:, :, 2 * R :] = jnp.zeros((4, 4, W - 2 * R, W), BF)

    barrier = pltpu.get_barrier_semaphore()
    partners = [at(k=1 - k)]
    for d in (1, 2, 3):
        partners += [at(zl=zl ^ d), at(y=y ^ d), at(zh=zh ^ d), at(x=x ^ d)]
    for device in partners:
        pl.semaphore_signal(barrier, inc=1, device_id=device, device_id_type=pl.DeviceIdType.MESH)
    pl.semaphore_wait(barrier, len(partners))

    mine = a_buf.at[rows_of(y)]
    for d in (1, 2, 3):
        to = zl ^ d
        send(mine, b_buf.at[zl, rows_of(k)], s_b.at[d], r_b.at[zl], at(zl=to))
    for d in (1, 3, 2):
        send(mine, mine, s_a.at[d], r_a.at[y], at(y=y ^ d))
    send(mine, b_buf.at[zl, rows_of(k)], s_c.at[0], r_c.at[zl], at(k=1 - k))
    for d in (1, 2, 3):
        f = y ^ d
        arrived(a_buf.at[rows_of(f)], s_a.at[d], r_a.at[f])

    def sum_x(d):
        t = zl ^ d
        total = gp[t, rows_of(x)].astype(F32)
        for e in (1, 2, 3):
            f = x ^ e
            arrived(rx.at[t, f], s_x.at[d, e], r_x.at[t, f])
            total += rx[t, f].astype(F32)
        zs[t] = total.astype(BF)

        @pl.when(t != zh)
        def _():
            copy = pltpu.make_async_remote_copy(
                src_ref=zs.at[t], dst_ref=rz.at[zh], send_sem=s_z.at[t], recv_sem=r_z.at[zh],
                device_id=at(zh=t), device_id_type=pl.DeviceIdType.MESH,
            )
            copy.start()

    for d in range(4):
        t = zl ^ d
        if d:
            arrived(b_buf.at[t, rows_of(k)], s_b.at[d], r_b.at[t])
            send(b_buf.at[t, rows_of(k)], b_buf.at[t, rows_of(k)], s_c.at[d], r_c.at[t], at(k=1 - k))
        arrived(b_buf.at[t, rows_of(1 - k)], s_c.at[d], r_c.at[t])
        gp[t] = dot_t(a_buf[...], b_buf[t]).astype(BF)
        for e in (1, 3, 2):
            to = x ^ e
            send(gp.at[t, rows_of(to)], rx.at[t, x], s_x.at[d, e], r_x.at[t, x], at(x=to))
        if d:
            sum_x(d - 1)
    sum_x(3)

    g = zs[zh].astype(F32)
    for e in (1, 2, 3):
        f = zh ^ e
        arrived(rz.at[f], s_z.at[f], r_z.at[f])
        g += rz[f].astype(F32)
    g_b = g.astype(BF)
    gs[...] = g_b
    gr[y, :, cols_of(zh)] = g_b
    gc[x, zl, rows_of(k)] = g_b
    for e in (1, 2, 3):
        to = zh ^ e
        pltpu.make_async_remote_copy(
            src_ref=zs.at[to], dst_ref=zs.at[to], send_sem=s_z.at[to], recv_sem=r_z.at[to],
            device_id=at(zh=to), device_id_type=pl.DeviceIdType.MESH,
        ).wait_send()

    for e in (1, 2, 3):
        send(gs, gr.at[y, :, cols_of(zh)], s_h.at[e], r_h.at[zh], at(zh=zh ^ e))
        send(gs, gc.at[x, zl, rows_of(k)], s_l.at[e], r_l.at[zl], at(zl=zl ^ e))
    for d in range(4):
        for (f, to_x) in [(zl ^ d, None)]:
            if d:
                arrived(gc.at[x, f, rows_of(k)], s_l.at[d], r_l.at[f])
            part = gc.at[x, f, rows_of(k)]
            for e in (1, 3, 2):
                send(part, part, s_q.at[d, e], r_q.at[x, f], at(x=x ^ e))
            send(part, part, s_k.at[0, d], r_k.at[x, f], at(k=1 - k))
        f = zh ^ d
        if d:
            arrived(gr.at[y, :, cols_of(f)], s_h.at[d], r_h.at[f])
        part = gr.at[y, :, cols_of(f)]
        for e in (1, 3, 2):
            send(part, part, s_y.at[d, e], r_y.at[y, f], at(y=y ^ e))
    for e in (1, 2, 3):
        for d in range(4):
            f, h = x ^ e, zl ^ d
            part = gc.at[f, h, rows_of(k)]
            arrived(part, s_q.at[d, e], r_q.at[f, h])
            send(part, part, s_k.at[e, d], r_k.at[f, h], at(k=1 - k))
    for e in range(4):
        for d in range(4):
            f, h = x ^ e, zl ^ d
            arrived(gc.at[f, h, rows_of(1 - k)], s_k.at[e, d], r_k.at[f, h])
    for e in (1, 2, 3):
        for d in range(4):
            f, h = y ^ e, zh ^ d
            arrived(gr.at[f, :, cols_of(h)], s_y.at[d, e], r_y.at[f, h])
    square = jnp.zeros((R, W), F32)
    for f in range(4):
        square += dot(gr[f], gc[f].reshape(4 * W, W))
    p_b = (-4.775 * g + 2.0315 * square).astype(BF)
    ps[...] = p_b
    pr[x, :, cols_of(zh)] = p_b

    for e in (1, 2, 3):
        send(ps, pr.at[x, :, cols_of(zh)], s_p.at[e], r_p.at[zh], at(zh=zh ^ e))
    for d in range(4):
        f = zh ^ d
        part = pr.at[x, :, cols_of(f)]
        if d:
            arrived(part, s_p.at[d], r_p.at[f])
        for e in (1, 3, 2):
            send(part, part, s_u.at[d, e], r_u.at[x, f], at(x=x ^ e))
    for e in range(4):
        f = x ^ e
        if e:
            for d in range(4):
                h = zh ^ d
                arrived(pr.at[f, :, cols_of(h)], s_u.at[d, e], r_u.at[f, h])
        osend[f] = dot(pr[f], b_buf[...].reshape(4 * W, C)).astype(BF)

        @pl.when(f != y)
        def _():
            pltpu.make_async_remote_copy(
                src_ref=osend.at[f], dst_ref=ro.at[y], send_sem=s_o.at[f], recv_sem=r_o.at[y],
                device_id=at(y=f), device_id_type=pl.DeviceIdType.MESH,
            ).start()

    total = 3.4445 * x_ref[...] + osend[y].astype(F32)
    for e in (1, 2, 3):
        f = y ^ e
        arrived(ro.at[f], s_o.at[f], r_o.at[f])
        total += ro[f].astype(F32)
    o_ref[...] = ((0.2 * math.sqrt(N)) * total).astype(BF)
    for e in (1, 2, 3):
        to = y ^ e
        pltpu.make_async_remote_copy(
            src_ref=osend.at[to], dst_ref=osend.at[to], send_sem=s_o.at[to], recv_sem=r_o.at[to],
            device_id=at(y=to), device_id_type=pl.DeviceIdType.MESH,
        ).wait_send()
    for copy in sent:
        copy.wait_send()


def body(iterate):
    dma = pltpu.SemaphoreType.DMA
    vmem = pl.BlockSpec(memory_space=pltpu.VMEM)
    one, two = dma((4,)), dma((4, 4))
    return pl.pallas_call(
        kernel,
        out_shape=jax.ShapeDtypeStruct((R, C), BF),
        in_specs=[vmem],
        out_specs=vmem,
        scratch_shapes=[
            pltpu.VMEM((4 * R, C), BF),
            pltpu.VMEM((4, W, C), BF),
            pltpu.VMEM((4, 4 * R, W), BF),
            pltpu.VMEM((4, 4, R, W), BF),
            pltpu.VMEM((4, R, W), BF),
            pltpu.VMEM((4, R, W), BF),
            pltpu.VMEM((R, W), BF),
            pltpu.VMEM((4, R, 4 * W), BF),
            pltpu.VMEM((4, 4, W, W), BF),
            pltpu.VMEM((4, R, 4 * W), BF),
            pltpu.VMEM((R, W), BF),
            pltpu.VMEM((4, R, C), BF),
            pltpu.VMEM((4, R, C), BF),
            one, one, one, one, one, one, two, two, one, one, one, one, two, two,
            one, one, two, two, two, two, one, one, two, two, one, one,
        ],
        compiler_params=pltpu.CompilerParams(
            collective_id=0, has_side_effects=True, vmem_limit_bytes=48 * 1024 * 1024
        ),
    )(iterate)


def solution(mesh):
    placed = (P("row", "col"),)
    return jax.shard_map(
        body, mesh=mesh, in_specs=placed, out_specs=P("row", "col"), check_vma=False
    )
```

time: 354 us -> 113 us (0.32); the launches traced: 349 us -> 113 us
  waiting for transfers between devices: 198 us -> 0 us
  blocking collectives: 122 us -> 0 us
  Pallas kernels: 0 us -> 112 us
  between operations: 13.1 us -> 0.01 us
  matrix products: 12.4 us -> 0 us
    all_gather x2 -> x0, blocking collectives: 122 us -> none  [the longest x1 62.3 us: body(): poly_column = lax.all_gather(poly, 'col', axis=0, tiled=True)]
    pallas_call x0 -> x1, Pallas kernels: none -> 112 us  [body(): pl.pallas_call(kernel, out_shape=jax.ShapeDtypeStruct((R, C), BF), in_spe...]
    reduce_scatter x1 -> x0, waiting for transfers between devices: 111 us -> none  [body(): lax.psum_scatter(partial_gram.astype(jnp.bfloat16), 'col', scatter_dimens...]
    all_gather x2 -> x0, waiting for transfers between devices: 86.8 us -> none  [the longest x1 78.5 us: body(): lax.all_gather(iterate_b, 'row', axis=0, tiled=True)]
    dot_general x3 -> x0, matrix products: 12.4 us -> none  [the longest x1 5.61 us: body(): lax.dot_general(lax.all_gather(iterate_b, 'row', axis=0, tiled=True), ite...]
  transfers between devices with their start and end apart: 3 -> 0, of which waited for: 3 -> 0; matrix products, arithmetic and copies ran while one was open for 0% -> 0% of each run, Pallas kernels for 0% -> 0%
where the time goes in v1:
time: 113 us
  Pallas kernels  112 us (99%)
  local copies, waits for them, and re-layouts  1.68 us (1%)
    pallas_call x1, Pallas kernels, body(): pl.pallas_call(kernel, out_shape=jax.ShapeDtypeStruct((R, C), BF), in_spe...  112 us

profile of v1, /device:TPU:1, one launch (start us, length us, event | category | flops | bytes accessed | tf_op | source)
XLA Modules:
  0.0 113.3 jit_solution(12819448151397972487)
XLA Ops:
  0.0 0.0 copy-start
  0.0 1.0 copy-done
  1.0 111.6 %shard_map.17 = bf16[112,896]{1,0:T(8,128)(2,1)S(1)} custom-call(f32[112,896]{1,0:T(8,128)S(1)} %copy-done), custom_call_target="tpu_custom_call" | custom-call | tf_op jit(solution)/shard_map/pallas_call | solution.py:217
  112.7 0.7 copy.3
Async XLA Ops:
  0.0 1.0 copy-start

commit v2 on v0

v2 whole, which is shorter than its diff:
```python
import math

import jax
import jax.numpy as jnp
from jax import lax
from jax.experimental import pallas as pl
from jax.experimental.pallas import tpu as pltpu
from jax.sharding import PartitionSpec as P

N = 14336
R = 112
C = 896
W = 256
HALF = 64
BF = jnp.bfloat16
F32 = jnp.float32
MESH = pl.DeviceIdType.MESH


def dot(a, b):
    return jnp.dot(a, b, preferred_element_type=F32)


def dot_t(a, b):
    return lax.dot_general(a, b, (((1,), (1,)), ((), ())), preferred_element_type=F32)


def rows_of(k):
    return pl.ds(pl.multiple_of(k * R, 16), R)


def cols_of(h):
    return pl.ds(pl.multiple_of(h * W, W), W)


def kernel(
    x_ref, o_ref,
    a_buf, xs, gp, rx, zs, rz, gs, gr, gc, pz, pr, acc,
    s_all, s_b, s_c, r_a, r_b, r_c, r_x, r_z, r_h, r_hh, r_y, r_l, r_q, r_k, r_p, r_ph, r_u, r_w, r_v,
):
    row = lax.axis_index("row")
    col = lax.axis_index("col")
    zl, y, k = row // 8, (row // 2) % 4, row % 2
    zh, x = col // 4, col % 4
    up, down, far = (zh + 1) % 4, (zh + 3) % 4, (zh + 2) % 4

    def at(zl=zl, y=y, k=k, zh=zh, x=x):
        return ((zl * 4 + y) * 2 + k, zh * 4 + x)

    sent = []

    def copy_of(src, dst, s, r, device):
        return pltpu.make_async_remote_copy(
            src_ref=src, dst_ref=dst, send_sem=s, recv_sem=r, device_id=device, device_id_type=MESH
        )

    def send(src, dst, r, device, when=None):
        copy = copy_of(src, dst, s_all.at[len(sent)], r, device)
        sent.append((copy, when))
        if when is None:
            copy.start()
        else:
            pl.when(when)(copy.start)

    def arrived(ref, r):
        pltpu.make_async_remote_copy(
            src_ref=ref, dst_ref=ref, send_sem=s_all.at[0], recv_sem=r,
            device_id=at(k=1 - k), device_id_type=MESH,
        ).wait_recv()

    barrier = pltpu.get_barrier_semaphore()
    partners = [at(k=1 - k)]
    for d in (1, 2, 3):
        partners += [at(zl=zl ^ d), at(y=y ^ d), at(zh=zh ^ d), at(x=x ^ d)]
    for device in partners:
        pl.semaphore_signal(barrier, inc=1, device_id=device, device_id_type=MESH)
    for f in range(4):

        @pl.when(jnp.logical_or(x != y, y != f))
        def _():
            pl.semaphore_signal(barrier, inc=1, device_id=at(x=y, y=f), device_id_type=MESH)

    x_b = x_ref[...].astype(BF)
    a_buf[rows_of(y)] = x_b
    xs[zl, y, rows_of(k)] = x_b
    xs[:, :, 2 * R :] = jnp.zeros((4, 4, W - 2 * R, C), BF)
    gc[:, :, 2 * R :] = jnp.zeros((4, 4, W - 2 * R, W), BF)
    pl.semaphore_wait(barrier, len(partners) + jnp.where(x == y, 3, 4))

    mine = a_buf.at[rows_of(y)]
    own = xs.at[zl, y, rows_of(k)]
    send(mine, own, r_b.at[zl], at(zl=jnp.minimum(zl + 1, 3)), zl < 3)
    send(mine, own, r_b.at[zl], at(zl=jnp.maximum(zl - 1, 0)), zl > 0)
    send(mine, own, r_c.at[zl], at(k=1 - k))
    for d in (1, 3, 2):
        send(mine, mine, r_a.at[y], at(y=y ^ d))

    def pick(table):
        t = jnp.where(zl == 0, table[0], table[1])
        return jnp.where(zl == 2, table[2], jnp.where(zl == 3, table[3], t))

    order = [zl, pick((1, 0, 1, 2)), pick((2, 2, 3, 1)), pick((3, 3, 0, 0))]
    middle = jnp.logical_and(zl > 0, zl < 3)

    def sum_x(t):
        total = gp[t, rows_of(x)].astype(F32)
        for e in (1, 3, 2):
            f = x ^ e
            arrived(rx.at[t, f], r_x.at[t, f])
            total += rx[t, f].astype(F32)
        zs[t] = total.astype(BF)
        send(zs.at[t], rz.at[zh], r_z.at[zh], at(zh=t), t != zh)

    def pass_on(t):
        part = xs.at[t, y, rows_of(k)]
        arrived(part, r_b.at[t])
        pl.when(middle)(line_copy(t).start)
        core_copy(t).start()

    def line_copy(t):
        part = xs.at[t, y, rows_of(k)]
        to = jnp.clip(jnp.where(t < zl, zl + 1, zl - 1), 0, 3)
        return copy_of(part, part, s_b.at[t], r_b.at[t], at(zl=to))

    def core_copy(t):
        part = xs.at[t, y, rows_of(k)]
        return copy_of(part, part, s_c.at[t], r_c.at[t], at(k=1 - k))

    def partial(t):
        arrived(xs.at[t, y, rows_of(1 - k)], r_c.at[t])
        gp[t] = dot_t(a_buf[...], xs[t, y]).astype(BF)
        for e in (1, 3, 2):
            to = x ^ e
            send(gp.at[t, rows_of(to)], rx.at[t, x], r_x.at[t, x], at(x=to))

    pass_on(order[1])
    pass_on(order[2])
    pl.when(middle)(lambda: pass_on(order[3]))
    for d in (1, 3, 2):
        arrived(a_buf.at[rows_of(y ^ d)], r_a.at[y ^ d])
    partial(order[0])
    partial(order[1])
    for t in order[1:3]:
        part = xs.at[t, y, rows_of(k)]
        for e in (1, 3, 2):
            send(part, part, r_w.at[t, y], at(y=y ^ e))
    sum_x(order[0])
    partial(order[2])
    sum_x(order[1])
    pl.when(jnp.logical_not(middle))(lambda: pass_on(order[3]))
    partial(order[3])
    part = xs.at[order[3], y, rows_of(k)]
    for e in (1, 3, 2):
        send(part, part, r_w.at[order[3], y], at(y=y ^ e))
    sum_x(order[2])
    sum_x(order[3])
    for t in order[1:]:
        pl.when(middle)(line_copy(t).wait_send)
        core_copy(t).wait_send()
        part = xs.at[t, y, rows_of(k)]

    g = zs[zh].astype(F32)
    for f in (up, down, far):
        arrived(rz.at[f], r_z.at[f])
        g += rz[f].astype(F32)
    g_b = g.astype(BF)
    gs[...] = g_b

    def ring(src, slot, r, rh, each, between=lambda: None):
        send(src, slot(zh, 0, R), r.at[zh], at(zh=up))
        send(src, slot(zh, 0, R), r.at[zh], at(zh=down))
        each(zh)
        between()
        arrived(slot(down, 0, R), r.at[down])
        send(slot(down, 0, HALF), slot(down, 0, HALF), rh.at[0], at(zh=up))
        each(down)
        arrived(slot(up, 0, R), r.at[up])
        send(slot(up, HALF, R - HALF), slot(up, HALF, R - HALF), rh.at[1], at(zh=down))
        each(up)

    gr[y, :, cols_of(zh)] = g_b
    gc[x, zl, rows_of(k)] = g_b

    def to_y(f):
        part = gr.at[y, :, cols_of(f)]
        for e in (1, 3, 2):
            send(part, part, r_y.at[y, f], at(y=y ^ e))

    def to_x(f):
        part = gc.at[x, f, rows_of(k)]
        for e in (1, 3, 2):
            send(part, part, r_q.at[x, f], at(x=x ^ e))

    def line():
        for e in (1, 2, 3):
            send(gs, gc.at[x, zl, rows_of(k)], r_l.at[zl], at(zl=zl ^ e))
        to_x(zl)

    def slot(f, start, size):
        return gr.at[y, pl.ds(start, size), cols_of(f)]

    ring(gs, slot, r_h, r_hh, to_y, line)
    for d in (1, 2, 3):
        f = zl ^ d
        arrived(gc.at[x, f, rows_of(k)], r_l.at[f])
        to_x(f)
    part = gc.at[x, :, rows_of(k)]
    send(part, part, r_k.at[x], at(k=1 - k))
    arrived(slot(far, 0, HALF), r_hh.at[0])
    arrived(slot(far, HALF, R - HALF), r_hh.at[1])
    to_y(far)
    for e in (1, 3, 2):
        f = x ^ e
        for h in range(4):
            arrived(gc.at[f, h, rows_of(k)], r_q.at[f, h])
        part = gc.at[f, :, rows_of(k)]
        send(part, part, r_k.at[f], at(k=1 - k))
    square = jnp.zeros((R, W), F32)
    for e in (0, 1, 3, 2):
        f = x ^ e
        arrived(gc.at[f, :, rows_of(1 - k)], r_k.at[f])
    for e in (0, 1, 3, 2):
        f = y ^ e
        if e:
            for h in range(4):
                arrived(gr.at[f, :, cols_of(h)], r_y.at[f, h])
        square += dot(gr[f], gc[f].reshape(4 * W, W))
    p_b = (-4.775 * g + 2.0315 * square).astype(BF)
    pz[zh] = p_b

    def spread(f):
        for e in range(4):
            to = x ^ e
            off = jnp.logical_or(to != x, x != y)
            send(pz.at[f], pr.at[f, :, cols_of(y)], r_u.at[f, y], at(x=to, y=x), off)

        @pl.when(x == y)
        def _():
            pr[f, :, cols_of(y)] = pz[f]

    def other_core():
        for e in (1, 3, 2):
            f = y ^ e
            xs[zl, f, rows_of(k)] = a_buf[rows_of(f)]
        for t in order:
            for e in (1, 3, 2):
                f = y ^ e
                part = xs.at[t, f, rows_of(k)]
                if t is not zl:
                    arrived(part, r_w.at[t, f])
                send(part, part, r_v.at[t, f], at(k=1 - k))

    ring(pz.at[zh], lambda f, start, size: pz.at[f, pl.ds(start, size)], r_p, r_ph, spread, other_core)
    arrived(pz.at[far, pl.ds(0, HALF)], r_ph.at[0])
    arrived(pz.at[far, pl.ds(HALF, R - HALF)], r_ph.at[1])
    spread(far)
    for t in order:
        for e in (1, 3, 2):
            f = y ^ e
            arrived(xs.at[t, f, rows_of(1 - k)], r_v.at[t, f])
    acc[...] = 3.4445 * x_ref[...]
    for f in (zh, down, up, far):
        for e in range(4):
            h = y ^ e

            @pl.when(jnp.logical_or(x != y, h != y))
            def _():
                arrived(pr.at[f, :, cols_of(h)], r_u.at[f, h])

        acc[...] += dot(pr[f], xs[f].reshape(4 * W, C))
    o_ref[...] = ((0.2 * math.sqrt(N)) * acc[...]).astype(BF)
    for copy, when in sent:
        if when is None:
            copy.wait_send()
        else:
            pl.when(when)(copy.wait_send)


def body(iterate):
    dma = pltpu.SemaphoreType.DMA
    vmem = pl.BlockSpec(memory_space=pltpu.VMEM)
    one, two = dma((4,)), dma((4, 4))
    return pl.pallas_call(
        kernel,
        out_shape=jax.ShapeDtypeStruct((R, C), BF),
        in_specs=[vmem],
        out_specs=vmem,
        scratch_shapes=[
            pltpu.VMEM((4 * R, C), BF),
            pltpu.VMEM((4, 4, W, C), BF),
            pltpu.VMEM((4, 4 * R, W), BF),
            pltpu.VMEM((4, 4, R, W), BF),
            pltpu.VMEM((4, R, W), BF),
            pltpu.VMEM((4, R, W), BF),
            pltpu.VMEM((R, W), BF),
            pltpu.VMEM((4, R, 4 * W), BF),
            pltpu.VMEM((4, 4, W, W), BF),
            pltpu.VMEM((4, R, W), BF),
            pltpu.VMEM((4, R, 4 * W), BF),
            pltpu.VMEM((R, C), F32),
            dma((128,)),
            one, one, one, one, one, two, one, one, one, two, one, two, one, one, one, two, two, two,
        ],
        compiler_params=pltpu.CompilerParams(
            collective_id=0, has_side_effects=True, vmem_limit_bytes=48 * 1024 * 1024
        ),
    )(iterate)


def solution(mesh):
    placed = (P("row", "col"),)
    return jax.shard_map(
        body, mesh=mesh, in_specs=placed, out_specs=P("row", "col"), check_vma=False
    )
```

time: 354 us -> 92.5 us (0.26); the launches traced: 349 us -> 91.7 us
  waiting for transfers between devices: 198 us -> 0 us
  blocking collectives: 122 us -> 0 us
  Pallas kernels: 0 us -> 90.1 us
  between operations: 13.1 us -> 0.01 us
  matrix products: 12.4 us -> 0 us
    all_gather x2 -> x0, blocking collectives: 122 us -> none  [the longest x1 62.3 us: body(): poly_column = lax.all_gather(poly, 'col', axis=0, tiled=True)]
    reduce_scatter x1 -> x0, waiting for transfers between devices: 111 us -> none  [body(): lax.psum_scatter(partial_gram.astype(jnp.bfloat16), 'col', scatter_dimens...]
    pallas_call x0 -> x1, Pallas kernels: none -> 90.1 us  [body(): pl.pallas_call(kernel, out_shape=jax.ShapeDtypeStruct((R, C), BF), in_spe...]
    all_gather x2 -> x0, waiting for transfers between devices: 86.8 us -> none  [the longest x1 78.5 us: body(): lax.all_gather(iterate_b, 'row', axis=0, tiled=True)]
    dot_general x3 -> x0, matrix products: 12.4 us -> none  [the longest x1 5.61 us: body(): lax.dot_general(lax.all_gather(iterate_b, 'row', axis=0, tiled=True), ite...]
  transfers between devices with their start and end apart: 3 -> 0, of which waited for: 3 -> 0; matrix products, arithmetic and copies ran while one was open for 0% -> 0% of each run, Pallas kernels for 0% -> 0%
where the time goes in v2:
time: 92.5 us; the launch traced here: 91.7 us
  Pallas kernels  90.1 us (97%)
  local copies, waits for them, and re-layouts  1.68 us (2%)
    pallas_call x1, Pallas kernels, body(): pl.pallas_call(kernel, out_shape=jax.ShapeDtypeStruct((R, C), BF), in_spe...  90.1 us

profile of v2, /device:TPU:1, one launch (start us, length us, event | category | flops | bytes accessed | tf_op | source)
XLA Modules:
  0.0 91.7 jit_solution(18121805491561841528)
XLA Ops:
  0.0 0.0 copy-start
  0.0 1.0 %copy-done = f32[112,896]{1,0:T(8,128)S(1)} copy-done((f32[112,896]{1,0:T(8,128)S(1)}, f32[112,896]{1,0:T(8,128)}, u32[]{:S(2)}) %copy-start) | copy-done | bytes 401432
  1.0 90.1 %shard_map.17 = bf16[112,896]{1,0:T(8,128)(2,1)S(1)} custom-call(f32[112,896]{1,0:T(8,128)S(1)} %copy-done), custom_call_target="tpu_custom_call" | custom-call | tf_op jit(solution)/shard_map/pallas_call | solution.py:283
  91.1 0.7 copy.3
Async XLA Ops:
  0.0 1.0 %copy-start = (f32[112,896]{1,0:T(8,128)S(1)}, f32[112,896]{1,0:T(8,128)}, u32[]{:S(2)}) copy-start(f32[112,896]{1,0:T(8,128)} %x_ref.1) | copy-start | bytes 1204228

commit v3 on v2

--- a/solution.py
+++ b/solution.py
@@ -35,14 +35,16 @@
 
 def kernel(
     x_ref, o_ref,
-    a_buf, xs, gp, rx, zs, rz, gs, gr, gc, pz, pr, acc,
-    s_all, s_b, s_c, r_a, r_b, r_c, r_x, r_z, r_h, r_hh, r_y, r_l, r_q, r_k, r_p, r_ph, r_u, r_w, r_v,
+    x_buf, a_buf, xs, gp, rx, zs, rz, gs, gr, gc, pz, pr, acc,
+    l_sem, s_all, s_b, s_c, r_a, r_b, r_c, r_x, r_z, r_h, r_hh, r_y, r_l, r_q, r_k, r_p, r_ph, r_u, r_w, r_v,
 ):
     row = lax.axis_index("row")
     col = lax.axis_index("col")
     zl, y, k = row // 8, (row // 2) % 4, row % 2
     zh, x = col // 4, col % 4
     up, down, far = (zh + 1) % 4, (zh + 3) % 4, (zh + 2) % 4
+    y_up, y_down, y_far = (y + 1) % 4, (y + 3) % 4, (y + 2) % 4
+    a_rows = (y, y_down, y_up, y_far)
 
     def at(zl=zl, y=y, k=k, zh=zh, x=x):
         return ((zl * 4 + y) * 2 + k, zh * 4 + x)
@@ -68,6 +70,9 @@
             device_id=at(k=1 - k), device_id_type=MESH,
         ).wait_recv()
 
+    load = pltpu.make_async_copy(x_ref, x_buf, l_sem)
+    load.start()
+
     barrier = pltpu.get_barrier_semaphore()
     partners = [at(k=1 - k)]
     for d in (1, 2, 3):
@@ -80,30 +85,31 @@
         def _():
             pl.semaphore_signal(barrier, inc=1, device_id=at(x=y, y=f), device_id_type=MESH)
 
-    x_b = x_ref[...].astype(BF)
-    a_buf[rows_of(y)] = x_b
+    load.wait()
+    x_b = x_buf[...].astype(BF)
+    a_buf[:R] = x_b
     xs[zl, y, rows_of(k)] = x_b
     xs[:, :, 2 * R :] = jnp.zeros((4, 4, W - 2 * R, C), BF)
     gc[:, :, 2 * R :] = jnp.zeros((4, 4, W - 2 * R, W), BF)
     pl.semaphore_wait(barrier, len(partners) + jnp.where(x == y, 3, 4))
 
-    mine = a_buf.at[rows_of(y)]
+    mine = a_buf.at[:R]
     own = xs.at[zl, y, rows_of(k)]
     send(mine, own, r_b.at[zl], at(zl=jnp.minimum(zl + 1, 3)), zl < 3)
     send(mine, own, r_b.at[zl], at(zl=jnp.maximum(zl - 1, 0)), zl > 0)
+    send(mine, a_buf.at[pl.ds(R, R)], r_a.at[0], at(y=y_up))
+    send(mine, a_buf.at[pl.ds(2 * R, R)], r_a.at[1], at(y=y_down))
     send(mine, own, r_c.at[zl], at(k=1 - k))
-    for d in (1, 3, 2):
-        send(mine, mine, r_a.at[y], at(y=y ^ d))
-
-    def pick(table):
-        t = jnp.where(zl == 0, table[0], table[1])
-        return jnp.where(zl == 2, table[2], jnp.where(zl == 3, table[3], t))
+
+    def pick(table, i=zl):
+        t = jnp.where(i == 0, table[0], table[1])
+        return jnp.where(i == 2, table[2], jnp.where(i == 3, table[3], t))
 
     order = [zl, pick((1, 0, 1, 2)), pick((2, 2, 3, 1)), pick((3, 3, 0, 0))]
     middle = jnp.logical_and(zl > 0, zl < 3)
 
     def sum_x(t):
-        total = gp[t, rows_of(x)].astype(F32)
+        total = gp[t, rows_of(pick((0, 2, 3, 1), (x + 4 - y) % 4))].astype(F32)
         for e in (1, 3, 2):
             f = x ^ e
             arrived(rx.at[t, f], r_x.at[t, f])
@@ -126,32 +132,43 @@
         part = xs.at[t, y, rows_of(k)]
         return copy_of(part, part, s_c.at[t], r_c.at[t], at(k=1 - k))
 
-    def partial(t):
+    def partial(t, parts):
+        lo, hi = parts[0], parts[-1] + 1
+        gp[t, lo * R : hi * R] = dot_t(a_buf[lo * R : hi * R], xs[t, y]).astype(BF)
+        for p in parts:
+            to = a_rows[p]
+            send(gp.at[t, pl.ds(p * R, R)], rx.at[t, x], r_x.at[t, x], at(x=to), to != x)
+
+    def slab_over_y(t):
+        part = xs.at[t, y, rows_of(k)]
+        for e in (1, 3, 2):
+            send(part, part, r_w.at[t, y], at(y=y ^ e))
+
+    def other_half(t):
         arrived(xs.at[t, y, rows_of(1 - k)], r_c.at[t])
-        gp[t] = dot_t(a_buf[...], xs[t, y]).astype(BF)
-        for e in (1, 3, 2):
-            to = x ^ e
-            send(gp.at[t, rows_of(to)], rx.at[t, x], r_x.at[t, x], at(x=to))
-
+
+    edge = jnp.logical_not(middle)
     pass_on(order[1])
-    pass_on(order[2])
+    pl.when(middle)(lambda: pass_on(order[2]))
+    arrived(a_buf.at[pl.ds(R, R)], r_a.at[0])
+    send(a_buf.at[pl.ds(R, 64)], a_buf.at[pl.ds(3 * R, 64)], r_a.at[2], at(y=y_up))
+    arrived(a_buf.at[pl.ds(2 * R, R)], r_a.at[1])
+    send(a_buf.at[pl.ds(2 * R + 64, 48)], a_buf.at[pl.ds(3 * R + 64, 48)], r_a.at[3], at(y=y_down))
+    arrived(a_buf.at[pl.ds(3 * R, 64)], r_a.at[2])
+    arrived(a_buf.at[pl.ds(3 * R + 64, 48)], r_a.at[3])
+    pl.when(edge)(lambda: pass_on(order[2]))
     pl.when(middle)(lambda: pass_on(order[3]))
-    for d in (1, 3, 2):
-        arrived(a_buf.at[rows_of(y ^ d)], r_a.at[y ^ d])
-    partial(order[0])
-    partial(order[1])
-    for t in order[1:3]:
-        part = xs.at[t, y, rows_of(k)]
-        for e in (1, 3, 2):
-            send(part, part, r_w.at[t, y], at(y=y ^ e))
+    for t in order[:3]:
+        other_half(t)
+        partial(t, (0, 1, 2, 3))
+    slab_over_y(order[1])
+    slab_over_y(order[2])
     sum_x(order[0])
-    partial(order[2])
+    pl.when(edge)(lambda: pass_on(order[3]))
     sum_x(order[1])
-    pl.when(jnp.logical_not(middle))(lambda: pass_on(order[3]))
-    partial(order[3])
-    part = xs.at[order[3], y, rows_of(k)]
-    for e in (1, 3, 2):
-        send(part, part, r_w.at[order[3], y], at(y=y ^ e))
+    other_half(order[3])
+    partial(order[3], (0, 1, 2, 3))
+    slab_over_y(order[3])
     sum_x(order[2])
     sum_x(order[3])
     for t in order[1:]:
@@ -191,34 +208,47 @@
         for e in (1, 3, 2):
             send(part, part, r_q.at[x, f], at(x=x ^ e))
 
-    def line():
-        for e in (1, 2, 3):
-            send(gs, gc.at[x, zl, rows_of(k)], r_l.at[zl], at(zl=zl ^ e))
-        to_x(zl)
-
     def slot(f, start, size):
         return gr.at[y, pl.ds(start, size), cols_of(f)]
 
-    ring(gs, slot, r_h, r_hh, to_y, line)
-    for d in (1, 2, 3):
+    def across(f, h):
+        part = gc.at[f, h, rows_of(k)]
+        send(part, part, r_k.at[f, h], at(k=1 - k))
+
+    def from_x(h):
+        for e in (1, 3, 2):
+            arrived(gc.at[x ^ e, h, rows_of(k)], r_q.at[x ^ e, h])
+            across(x ^ e, h)
+
+    send(gs, slot(zh, 0, R), r_h.at[zh], at(zh=up))
+    send(gs, slot(zh, 0, R), r_h.at[zh], at(zh=down))
+    for e in (1, 3, 2):
+        send(gs, gc.at[x, zl, rows_of(k)], r_l.at[zl], at(zl=zl ^ e))
+    to_x(zl)
+    to_y(zh)
+    across(x, zl)
+    for d in (1, 3, 2):
         f = zl ^ d
         arrived(gc.at[x, f, rows_of(k)], r_l.at[f])
         to_x(f)
-    part = gc.at[x, :, rows_of(k)]
-    send(part, part, r_k.at[x], at(k=1 - k))
+        across(x, f)
+    arrived(slot(down, 0, R), r_h.at[down])
+    send(slot(down, 0, HALF), slot(down, 0, HALF), r_hh.at[0], at(zh=up))
+    to_y(down)
+    arrived(slot(up, 0, R), r_h.at[up])
+    send(slot(up, HALF, R - HALF), slot(up, HALF, R - HALF), r_hh.at[1], at(zh=down))
+    to_y(up)
+    from_x(zl)
+    from_x(zl ^ 1)
+    from_x(zl ^ 3)
     arrived(slot(far, 0, HALF), r_hh.at[0])
     arrived(slot(far, HALF, R - HALF), r_hh.at[1])
     to_y(far)
-    for e in (1, 3, 2):
-        f = x ^ e
-        for h in range(4):
-            arrived(gc.at[f, h, rows_of(k)], r_q.at[f, h])
-        part = gc.at[f, :, rows_of(k)]
-        send(part, part, r_k.at[f], at(k=1 - k))
+    from_x(zl ^ 2)
     square = jnp.zeros((R, W), F32)
     for e in (0, 1, 3, 2):
-        f = x ^ e
-        arrived(gc.at[f, :, rows_of(1 - k)], r_k.at[f])
+        for d in (0, 1, 3, 2):
+            arrived(gc.at[x ^ e, zl ^ d, rows_of(1 - k)], r_k.at[x ^ e, zl ^ d])
     for e in (0, 1, 3, 2):
         f = y ^ e
         if e:
@@ -239,9 +269,8 @@
             pr[f, :, cols_of(y)] = pz[f]
 
     def other_core():
-        for e in (1, 3, 2):
-            f = y ^ e
-            xs[zl, f, rows_of(k)] = a_buf[rows_of(f)]
+        for p in (1, 2, 3):
+            xs[zl, a_rows[p], rows_of(k)] = a_buf[p * R : (p + 1) * R]
         for t in order:
             for e in (1, 3, 2):
                 f = y ^ e
@@ -250,7 +279,8 @@
                     arrived(part, r_w.at[t, f])
                 send(part, part, r_v.at[t, f], at(k=1 - k))
 
-    ring(pz.at[zh], lambda f, start, size: pz.at[f, pl.ds(start, size)], r_p, r_ph, spread, other_core)
+    ring(pz.at[zh], lambda f, start, size: pz.at[f, pl.ds(start, size)], r_p, r_ph, spread)
+    other_core()
     arrived(pz.at[far, pl.ds(0, HALF)], r_ph.at[0])
     arrived(pz.at[far, pl.ds(HALF, R - HALF)], r_ph.at[1])
     spread(far)
@@ -258,7 +288,7 @@
         for e in (1, 3, 2):
             f = y ^ e
             arrived(xs.at[t, f, rows_of(1 - k)], r_v.at[t, f])
-    acc[...] = 3.4445 * x_ref[...]
+    acc[...] = 3.4445 * x_buf[...]
     for f in (zh, down, up, far):
         for e in range(4):
             h = y ^ e
@@ -283,9 +313,10 @@
     return pl.pallas_call(
         kernel,
         out_shape=jax.ShapeDtypeStruct((R, C), BF),
-        in_specs=[vmem],
+        in_specs=[pl.BlockSpec(memory_space=pl.ANY)],
         out_specs=vmem,
         scratch_shapes=[
+            pltpu.VMEM((R, C), F32),
             pltpu.VMEM((4 * R, C), BF),
             pltpu.VMEM((4, 4, W, C), BF),
             pltpu.VMEM((4, 4 * R, W), BF),
@@ -298,8 +329,9 @@
             pltpu.VMEM((4, R, W), BF),
             pltpu.VMEM((4, R, 4 * W), BF),
             pltpu.VMEM((R, C), F32),
+            dma(()),
             dma((128,)),
-            one, one, one, one, one, two, one, one, one, two, one, two, one, one, one, two, two, two,
+            one, one, one, one, one, two, one, one, one, two, one, two, two, one, one, two, two, two,
         ],
         compiler_params=pltpu.CompilerParams(
             collective_id=0, has_side_effects=True, vmem_limit_bytes=48 * 1024 * 1024

time: 92.5 us -> 90.7 us (0.981)
  the two profiles are of different devices: /device:TPU:1 before, /device:TPU:16 now
where the time goes in v3:
time: 90.7 us; the launch traced here: 90.5 us
  Pallas kernels  88.8 us (98%)
  local copies, waits for them, and re-layouts  1.68 us (2%)
    pallas_call x1, Pallas kernels, body(): pl.pallas_call(kernel, out_shape=jax.ShapeDtypeStruct((R, C), BF), in_spe...  88.8 us

profile of v3, /device:TPU:16, one launch (start us, length us, event | category | flops | bytes accessed | tf_op | source)
XLA Modules:
  0.0 90.5 jit_solution(1345806010369473715)
XLA Ops:
  0.0 0.0 copy-start
  0.0 1.0 %copy-done = f32[112,896]{1,0:T(8,128)S(1)} copy-done((f32[112,896]{1,0:T(8,128)S(1)}, f32[112,896]{1,0:T(8,128)}, u32[]{:S(2)}) %copy-start) | copy-done | bytes 401432
  1.0 88.8 %shard_map.17 = bf16[112,896]{1,0:T(8,128)(2,1)S(1)} custom-call(f32[112,896]{1,0:T(8,128)S(1)} %copy-done), custom_call_target="tpu_custom_call" | custom-call | tf_op jit(solution)/shard_map/pallas_call | solution.py:313
  89.9 0.7 copy.3
Async XLA Ops:
  0.0 1.0 %copy-start = (f32[112,896]{1,0:T(8,128)S(1)}, f32[112,896]{1,0:T(8,128)}, u32[]{:S(2)}) copy-start(f32[112,896]{1,0:T(8,128)} %x_ref.1) | copy-start | bytes 1204228

commit v4 on v3

--- a/solution.py
+++ b/solution.py
@@ -35,7 +35,7 @@
 
 def kernel(
     x_ref, o_ref,
-    x_buf, a_buf, xs, gp, rx, zs, rz, gs, gr, gc, pz, pr, acc,
+    x_buf, a_buf, xs, gp, rx, zs, rz, gs, gr, gc, pz, pr,
     l_sem, s_all, s_b, s_c, r_a, r_b, r_c, r_x, r_z, r_h, r_hh, r_y, r_l, r_q, r_k, r_p, r_ph, r_u, r_w, r_v,
 ):
     row = lax.axis_index("row")
@@ -288,7 +288,7 @@
         for e in (1, 3, 2):
             f = y ^ e
             arrived(xs.at[t, f, rows_of(1 - k)], r_v.at[t, f])
-    acc[...] = 3.4445 * x_buf[...]
+    o_ref[...] = 3.4445 * x_buf[...]
     for f in (zh, down, up, far):
         for e in range(4):
             h = y ^ e
@@ -297,8 +297,7 @@
             def _():
                 arrived(pr.at[f, :, cols_of(h)], r_u.at[f, h])
 
-        acc[...] += dot(pr[f], xs[f].reshape(4 * W, C))
-    o_ref[...] = ((0.2 * math.sqrt(N)) * acc[...]).astype(BF)
+        o_ref[...] += dot(pr[f], xs[f].reshape(4 * W, C))
     for copy, when in sent:
         if when is None:
             copy.wait_send()
@@ -310,9 +309,9 @@
     dma = pltpu.SemaphoreType.DMA
     vmem = pl.BlockSpec(memory_space=pltpu.VMEM)
     one, two = dma((4,)), dma((4, 4))
-    return pl.pallas_call(
+    total = pl.pallas_call(
         kernel,
-        out_shape=jax.ShapeDtypeStruct((R, C), BF),
+        out_shape=jax.ShapeDtypeStruct((R, C), F32),
         in_specs=[pl.BlockSpec(memory_space=pl.ANY)],
         out_specs=vmem,
         scratch_shapes=[
@@ -328,7 +327,6 @@
             pltpu.VMEM((4, 4, W, W), BF),
             pltpu.VMEM((4, R, W), BF),
             pltpu.VMEM((4, R, 4 * W), BF),
-            pltpu.VMEM((R, C), F32),
             dma(()),
             dma((128,)),
             one, one, one, one, one, two, one, one, one, two, one, two, two, one, one, two, two, two,
@@ -337,6 +335,7 @@
             collective_id=0, has_side_effects=True, vmem_limit_bytes=48 * 1024 * 1024
         ),
     )(iterate)
+    return ((0.2 * math.sqrt(N)) * total).astype(BF)
 
 
 def solution(mesh):

time: 90.7 us -> 90.7 us (level)
  no operation moved by 1% of the time
where the time goes in v4:
time: 90.7 us; the launch traced here: 90.6 us
  Pallas kernels  88.8 us (98%)
  local copies, waits for them, and re-layouts  1 us (1%)
    pallas_call x1, Pallas kernels, body(): pl.pallas_call(kernel, out_shape=jax.ShapeDtypeStruct((R, C), F32), in_sp...  88.8 us

profile of v4, /device:TPU:16, one launch (start us, length us, event | category | flops | bytes accessed | tf_op | source)
XLA Modules:
  0.0 90.6 jit_solution(3936368792888677795)
XLA Ops:
  0.0 0.0 copy-start
  0.0 1.0 %copy-done = f32[112,896]{1,0:T(8,128)S(1)} copy-done((f32[112,896]{1,0:T(8,128)S(1)}, f32[112,896]{1,0:T(8,128)}, u32[]{:S(2)}) %copy-start) | copy-done | bytes 401432
  1.0 88.8 %shard_map.17 = f32[112,896]{1,0:T(8,128)S(1)} custom-call(f32[112,896]{1,0:T(8,128)S(1)} %copy-done), custom_call_target="tpu_custom_call" | custom-call | tf_op jit(solution)/shard_map/pallas_call | solution.py:312
  89.9 0.7 multiply_convert_fusion
Async XLA Ops:
  0.0 1.0 %copy-start = (f32[112,896]{1,0:T(8,128)S(1)}, f32[112,896]{1,0:T(8,128)}, u32[]{:S(2)}) copy-start(f32[112,896]{1,0:T(8,128)} %x_ref.1) | copy-start | bytes 1204228

commit v5 on v4

--- a/solution.py
+++ b/solution.py
@@ -11,7 +11,6 @@
 R = 112
 C = 896
 W = 256
-HALF = 64
 BF = jnp.bfloat16
 F32 = jnp.float32
 MESH = pl.DeviceIdType.MESH
@@ -189,10 +188,10 @@
         each(zh)
         between()
         arrived(slot(down, 0, R), r.at[down])
-        send(slot(down, 0, HALF), slot(down, 0, HALF), rh.at[0], at(zh=up))
+        send(slot(down, 0, R), slot(down, 0, R), rh.at[0], at(zh=up), zl % 2 == 0)
         each(down)
         arrived(slot(up, 0, R), r.at[up])
-        send(slot(up, HALF, R - HALF), slot(up, HALF, R - HALF), rh.at[1], at(zh=down))
+        send(slot(up, 0, R), slot(up, 0, R), rh.at[0], at(zh=down), zl % 2 == 1)
         each(up)
 
     gr[y, :, cols_of(zh)] = g_b
@@ -233,16 +232,15 @@
         to_x(f)
         across(x, f)
     arrived(slot(down, 0, R), r_h.at[down])
-    send(slot(down, 0, HALF), slot(down, 0, HALF), r_hh.at[0], at(zh=up))
+    send(slot(down, 0, R), slot(down, 0, R), r_hh.at[0], at(zh=up), zl % 2 == 0)
     to_y(down)
     arrived(slot(up, 0, R), r_h.at[up])
-    send(slot(up, HALF, R - HALF), slot(up, HALF, R - HALF), r_hh.at[1], at(zh=down))
+    send(slot(up, 0, R), slot(up, 0, R), r_hh.at[0], at(zh=down), zl % 2 == 1)
     to_y(up)
     from_x(zl)
     from_x(zl ^ 1)
     from_x(zl ^ 3)
-    arrived(slot(far, 0, HALF), r_hh.at[0])
-    arrived(slot(far, HALF, R - HALF), r_hh.at[1])
+    arrived(slot(far, 0, R), r_hh.at[0])
     to_y(far)
     from_x(zl ^ 2)
     square = jnp.zeros((R, W), F32)
@@ -281,8 +279,7 @@
 
     ring(pz.at[zh], lambda f, start, size: pz.at[f, pl.ds(start, size)], r_p, r_ph, spread)
     other_core()
-    arrived(pz.at[far, pl.ds(0, HALF)], r_ph.at[0])
-    arrived(pz.at[far, pl.ds(HALF, R - HALF)], r_ph.at[1])
+    arrived(pz.at[far], r_ph.at[0])
     spread(far)
     for t in order:
         for e in (1, 3, 2):

time: 90.7 us -> 91.2 us (level)
  the two profiles are of different devices: /device:TPU:16 before, /device:TPU:1 now
where the time goes in v5:
time: 91.2 us; the launch traced here: 90.5 us
  Pallas kernels  88.8 us (97%)
  local copies, waits for them, and re-layouts  1 us (1%)
    pallas_call x1, Pallas kernels, body(): pl.pallas_call(kernel, out_shape=jax.ShapeDtypeStruct((R, C), F32), in_sp...  88.8 us

profile of v5, /device:TPU:1, one launch (start us, length us, event | category | flops | bytes accessed | tf_op | source)
XLA Modules:
  0.0 90.5 jit_solution(2672640616553813949)
XLA Ops:
  0.0 0.0 copy-start
  0.0 1.0 %copy-done = f32[112,896]{1,0:T(8,128)S(1)} copy-done((f32[112,896]{1,0:T(8,128)S(1)}, f32[112,896]{1,0:T(8,128)}, u32[]{:S(2)}) %copy-start) | copy-done | bytes 401432
  1.0 88.8 %shard_map.17 = f32[112,896]{1,0:T(8,128)S(1)} custom-call(f32[112,896]{1,0:T(8,128)S(1)} %copy-done), custom_call_target="tpu_custom_call" | custom-call | tf_op jit(solution)/shard_map/pallas_call | solution.py:309
  89.8 0.7 multiply_convert_fusion
Async XLA Ops:
  0.0 1.0 %copy-start = (f32[112,896]{1,0:T(8,128)S(1)}, f32[112,896]{1,0:T(8,128)}, u32[]{:S(2)}) copy-start(f32[112,896]{1,0:T(8,128)} %x_ref.1) | copy-start | bytes 1204228
